TPU v7x, 512 devices: a whole 4x8x8 slice. The times are simulated.
512 devices in a mesh: loop: 16 (over y, x_hi), dp: 32 (over z, x_lo, core).
Axes of the slice: x: 4 (x_hi: 2, x_lo: 2; x = x_hi * 2 + x_lo), y: 8, z: 8, core: 2. Of those that a mesh axis runs over, the one named last changes fastest.
Arguments:
- images: bfloat16 [32, 32, 16, 16, 768], P('dp', 'loop'), may hold values from -6 to 6
- kernel: float32 [7, 7, 768], replicated, may hold values from -0.875 to 0.875
- ln_gain: float32 [768], replicated, may hold values from 0.5 to 1.5
- w_up: bfloat16 [768, 1536], P('dp'), may hold values from -0.21875 to 0.21875
- b_up: float32 [1536], replicated, may hold values from -3 to 3
- w_down: bfloat16 [1536, 768], P('dp'), may hold values from -0.15625 to 0.15625
- layer_scale: float32 [768], replicated, may hold values from 0.3 to 1
- w_head: bfloat16 [768, 1152], P('dp'), may hold values from -0.21875 to 0.21875
- text_rows: bfloat16 [32, 32, 1152], P('dp', 'loop'), may hold values from -6 to 6
- pair_ids: int32 [32, 32], P('dp', 'loop'), may hold values from 0 to 31, each once within a row
- log_temp: float32 [1], replicated, may hold values from 1.5 to 2.5
- loss_bias: float32 [1], replicated, may hold values from -6 to -2
Outputs:
- kernel_grad: float32 [7, 7, 768], replicated
- up_grad: float32 [768, 1536], P('dp')
- text_grad: float32 [32, 32, 1152], P('dp', 'loop')
Inputs may be any that keep to these rules, and one draw needn't show every extreme that they name: Each row of pair_ids holds every index of its group once.
All inputs are finite; a program needn't handle non-finite values.
Results may differ from a plain program's by a relative error of at most 0.04.
Values may be sent and summed in bfloat16 or wider, within the bound.
A program may use at most 64 MiB of HBM per device.

v0:
```python
import jax
import jax.numpy as jnp
from jax import lax
from jax.sharding import PartitionSpec as P

epsilon = 1e-06


def passed_along(value, axis, steps):
    count = lax.axis_size(axis)
    pairs = [(source, (source + steps) % count) for source in range(count)]
    return lax.ppermute(value, axis, pairs)


def image_tower(kernel, w_up, images, ln_gain, b_up, w_down, layer_scale, w_head):
    image_count = images.shape[0]
    grid_side = images.shape[1]
    channels = images.shape[3]
    padded = jnp.pad(images, ((0, 0), (3, 3), (3, 3), (0, 0)))
    conv_out = jnp.zeros(images.shape, jnp.float32)
    for row_off in range(7):
        for col_off in range(7):
            window = padded[:, row_off : row_off + grid_side, col_off : col_off + grid_side, :]
            conv_out = conv_out + window.astype(jnp.float32) * kernel[row_off, col_off]
    chan_mean = jnp.mean(conv_out, axis=-1, keepdims=True)
    centered = conv_out - chan_mean
    chan_var = jnp.mean(centered * centered, axis=-1, keepdims=True)
    normed = (centered * lax.rsqrt(chan_var + epsilon) * ln_gain).astype(jnp.bfloat16)
    flat_rows = normed.reshape(-1, channels)
    hidden = jnp.dot(flat_rows, w_up, preferred_element_type=jnp.float32) + b_up
    active = jax.nn.gelu(hidden, approximate=True).astype(jnp.bfloat16)
    mlp_out = jnp.dot(active, w_down, preferred_element_type=jnp.float32)
    block_out = images.reshape(-1, channels).astype(jnp.float32) + layer_scale * mlp_out
    pooled = jnp.mean(
        block_out.reshape(image_count, grid_side * grid_side, channels), axis=1
    ).astype(jnp.bfloat16)
    embedding = jnp.dot(pooled, w_head, preferred_element_type=jnp.float32)
    return embedding * lax.rsqrt(jnp.sum(embedding * embedding, axis=-1, keepdims=True) + epsilon)


def pair_grad(image_emb, text_emb, pair_row, text_index, logit_scale, logit_bias, group_size):
    logits = (
        logit_scale * jnp.dot(image_emb, text_emb.T, precision=lax.Precision.HIGHEST) + logit_bias
    )
    sign_of = jnp.where(pair_row[:, None] == text_index[None, :], 1.0, -1.0)
    return -sign_of * jax.nn.sigmoid(-sign_of * logits) / group_size


def body(
    images,
    kernel,
    ln_gain,
    w_up,
    b_up,
    w_down,
    layer_scale,
    w_head,
    text_rows,
    pair_ids,
    log_temp,
    loss_bias,
):
    loop_size = lax.axis_size("loop")
    loop_index = lax.axis_index("loop")
    up_full, down_full, head_full = (
        lax.all_gather(w_up, "dp", axis=0, tiled=True),
        lax.all_gather(w_down, "dp", axis=0, tiled=True),
        lax.all_gather(w_head, "dp", axis=0, tiled=True),
    )
    pictures = images[0]
    pair_row = pair_ids[0]
    img_dev = pictures.shape[0]
    group_size = img_dev * loop_size
    logit_scale = jnp.exp(log_temp[0])
    logit_bias = loss_bias[0]

    def run_tower(kernel_arg, up_arg):
        return image_tower(
            kernel_arg, up_arg, pictures, ln_gain, b_up, down_full, layer_scale, head_full
        )

    image_emb, pullback = jax.vjp(run_tower, kernel, up_full)
    raw_rows = text_rows[0].astype(jnp.float32)
    text_norm = jnp.sqrt(jnp.sum(raw_rows * raw_rows, axis=-1, keepdims=True) + epsilon)
    text_hat = raw_rows / text_norm
    rounded = lax.optimization_barrier(text_hat.astype(jnp.bfloat16))
    local_index = jnp.arange(img_dev, dtype=jnp.int32)

    def cycle_step(step_index, state):
        text_block, partials, image_cot = state
        source = (loop_index - step_index) % loop_size
        text_index = source * img_dev + local_index
        pair_weight = pair_grad(
            image_emb, text_block, pair_row, text_index, logit_scale, logit_bias, group_size
        )
        image_cot = image_cot + logit_scale * jnp.dot(
            pair_weight, text_block, precision=lax.Precision.HIGHEST
        )
        partials = partials + logit_scale * jnp.dot(
            pair_weight.T, image_emb, precision=lax.Precision.HIGHEST
        )
        text_block, partials = passed_along((text_block, partials), "loop", 1)
        return (text_block, partials, image_cot)

    start = (
        rounded.astype(jnp.float32),
        jnp.zeros(raw_rows.shape, jnp.float32),
        jnp.zeros(image_emb.shape, jnp.float32),
    )
    _, text_cot, image_cot = lax.fori_loop(0, loop_size, cycle_step, start)
    text_grad = (
        text_cot - text_hat * jnp.sum(text_hat * text_cot, axis=-1, keepdims=True)
    ) / text_norm
    kernel_part, up_part = pullback(image_cot)
    kernel_grad = lax.psum(kernel_part, ("loop", "dp"))
    up_rows = lax.psum_scatter(
        up_part.astype(jnp.float32).astype(jnp.bfloat16), "dp", scatter_dimension=0, tiled=True
    )
    up_grad = lax.psum(up_rows, "loop").astype(jnp.float32)
    return (kernel_grad, up_grad, text_grad[None])


def solution(mesh):
    placed = (
        P("dp", "loop", None, None, None),
        P(),
        P(),
        P("dp", None),
        P(),
        P("dp", None),
        P(),
        P("dp", None),
        P("dp", "loop", None),
        P("dp", "loop"),
        P(),
        P(),
    )
    return jax.shard_map(
        body,
        mesh=mesh,
        in_specs=placed,
        out_specs=(P(), P("dp", None), P("dp", "loop", None)),
        check_vma=False,
    )
```

profile of v0, /device:TPU:1, one launch (start us, length us, event | category | flops | bytes accessed | tf_op | source)
XLA Modules:
  0.0 996.5 jit_solution(3485320233537033907)
XLA Ops:
  15.5 30.5 %fusion.140 = (f32[2,16,16]{2,1,0:T(8,128)S(1)}, f32[2,16,16,768]{3,2,1,0:T(8,128)S(1)}) fusion(f32[768]{0:T(1024)S(1)} %get-tuple-element.377, f32[768]{0:T(1024)S(1)} %get-tuple-element.378, f32[768]{0:T(1024)S(1)} %get-tuple-element.331, f32[768]{0:T(1024)S(1)} %get-tuple-element.332, f32[768]{0:T(1024)S(1)} %get-tuple-element.333, ...), kind=kLoop, calls=%fused_computation.374 | loop fusion | flops 57802240 | bytes 2511872 | tf_op jit(solution)/shard_map/jvp()/reduce_sum | solution.py:25
  46.7 37.7 %all-gather.4.cloned.1.call-done = bf16[768,1536]{1,0:T(8,128)(2,1)} async-done(((bf16[24,1536]{1,0:T(8,128)(2,1)}), bf16[768,1536]{1,0:T(8,128)(2,1)}) %all-gather.4.cloned.1.call-update) | async-done | bytes 2359312 | tf_op jit(solution)/shard_map/all_gather | solution.py:66
  84.4 4.8 convolution_add_fusion
  89.2 65.1 %all-gather.6.cloned.1.call-done = bf16[1536,768]{1,0:T(8,128)(2,1)} async-done(((bf16[48,768]{1,0:T(8,128)(2,1)}), bf16[1536,768]{1,0:T(8,128)(2,1)}) %all-gather.6.cloned.1.call-update) | async-done | bytes 2359312 | tf_op jit(solution)/shard_map/all_gather | solution.py:67
  154.3 4.6 bitcast_reduce_fusion
  158.9 64.5 %all-gather.8.cloned.1.call-done = bf16[768,1152]{1,0:T(8,128)(2,1)} async-done(((bf16[24,1152]{1,0:T(8,128)(2,1)}), bf16[768,1152]{1,0:T(8,128)(2,1)}) %all-gather.8.cloned.1.call-update) | async-done | bytes 1769488 | tf_op jit(solution)/shard_map/all_gather | solution.py:68
  225.4 184.7 %while.20 = (s32[]{:T(128)}, f32[2,1152]{1,0:T(2,128)S(1)}, f32[2,1152]{1,0:T(2,128)S(1)}, f32[2,1152]{1,0:T(2,128)S(1)}, f32[]{:T(128)}, /*index=5*/s32[1,2]{1,...) while((s32[]{:T(128)}, f32[2,1152]{1,0:T(2,128)S(1)}, ...), condition=%wide.region_6.7_spmd.clone, body=%wide.region_5.6_spmd.clone.sunk | while | flops 177470 | bytes 166336 | solution.py:110
  225.5 4.3 collective-permute-start
  230.9 3.4 collective-permute-start.1
  234.5 4.4 collective-permute-done.1
  242.0 4.6 collective-permute-start.1
  246.8 3.2 collective-permute-done.1
  253.7 3.4 collective-permute-start.1
  257.3 4.4 collective-permute-done.1
  264.8 4.6 collective-permute-start.1
  269.5 3.2 collective-permute-done.1
  276.4 3.4 collective-permute-start.1
  280.0 4.4 collective-permute-done.1
  287.5 4.6 collective-permute-start.1
  292.3 3.2 collective-permute-done.1
  299.1 5.2 collective-permute-start.1
  307.1 3.1 collective-permute-start
  311.4 6.0 collective-permute-start.1
  319.4 3.9 collective-permute-start
  324.4 3.9 collective-permute-start.1
  328.5 4.0 collective-permute-done.1
  335.6 3.8 collective-permute-start.1
  339.6 4.1 collective-permute-done.1
  346.7 3.8 collective-permute-start.1
  350.7 4.1 collective-permute-done.1
  357.8 3.8 collective-permute-start.1
  361.8 4.1 collective-permute-done.1
  368.9 3.8 collective-permute-start.1
  372.8 4.1 collective-permute-done.1
  380.0 3.8 collective-permute-start.1
  384.0 4.0 collective-permute-done.1
  391.1 3.8 collective-permute-start.1
  395.0 4.1 collective-permute-done.1
  402.2 4.1 collective-permute-start.1
  406.5 3.7 collective-permute-done.1
  412.6 4.6 fusion.14
  421.3 3.6 fusion.143
  426.0 5.0 fusion.117
  431.1 3.7 fusion.23
  434.9 3.9 fusion.118
  440.1 119.1 %reduce-scatter.2.cloned.1.call-done = bf16[24,1536]{1,0:T(8,128)(2,1)} async-done(((bf16[768,1536]{1,0:T(8,128)(2,1)}), bf16[24,1536]{1,0:T(8,128)(2,1)}) %reduce-scatter.2.cloned.1.call-update) | async-done | bytes 73744 | tf_op jit(solution)/shard_map/reduce_scatter | solution.py:116
  560.5 148.9 %all-reduce.55.cloned.1.call-done = bf16[24,1536]{1,0:T(8,128)(2,1)} async-done(((bf16[24,1536]{1,0:T(8,128)(2,1)}), bf16[24,1536]{1,0:T(8,128)(2,1)}) %all-reduce.55.cloned.1.call-update) | async-done | bytes 73744 | tf_op jit(solution)/shard_map/psum | solution.py:119
  711.0 277.1 %all-reduce.53.cloned.1.call-done = f32[7,7,768]{2,1,0:T(8,128)} async-done(((f32[7,7,768]{2,1,0:T(8,128)}), f32[7,7,768]{2,1,0:T(8,128)}) %all-reduce.53.cloned.1.call-update) | async-done | bytes 150544 | tf_op jit(solution)/shard_map/psum | solution.py:115
  (216 shorter events, 74.9 us)
Async XLA Ops:
  7.2 77.2 %all-gather.4.cloned.1.call-start = ((), (), s32[]{:S(2)}) async-start(), calls=%async_computation.1 | async-start | bytes 2433024 | tf_op jit(solution)/shard_map/all_gather | solution.py:66
  7.9 146.4 %all-gather.6.cloned.1.call-start = ((), (), s32[]{:S(2)}) async-start(), calls=%async_computation.2 | async-start | bytes 2433024 | tf_op jit(solution)/shard_map/all_gather | solution.py:67
  8.6 214.8 %all-gather.8.cloned.1.call-start = ((), (), s32[]{:S(2)}) async-start(), calls=%async_computation.3 | async-start | bytes 1824768 | tf_op jit(solution)/shard_map/all_gather | solution.py:68
  9.4 549.9 %reduce-scatter.2.cloned.1.call-start = ((), (), s32[]{:S(2)}) async-start(), calls=%async_computation.5 | async-start | bytes 2433024 | tf_op jit(solution)/shard_map/reduce_scatter | solution.py:116
  15.5 30.9 %copy-start.1 = (f32[768]{0:T(1024)S(1)}, f32[768]{0:T(1024)}, u32[]{:S(2)}) copy-start(f32[768]{0:T(1024)} %param.16) | copy-start | bytes 9220
  46.4 38.0 %copy-start.4 = (f32[1536]{0:T(1024)S(1)}, f32[1536]{0:T(1024)}, u32[]{:S(2)}) copy-start(f32[1536]{0:T(1024)} %param.18) | copy-start | bytes 18436
  84.4 69.9 %copy-start = (bf16[1,2,16,16,768]{4,3,2,1,0:T(8,128)(2,1)S(1)}, bf16[1,2,16,16,768]{4,3,2,1,0:T(8,128)(2,1)}, u32[]{:S(2)}) copy-start(bf16[1,2,16,16,768]{4,3,2,1,0:T(8,128)(2,1)} %param.14) | copy-start | bytes 2359300
  84.4 69.9 %copy-start.2 = (f32[768]{0:T(1024)S(1)}, f32[768]{0:T(1024)}, u32[]{:S(2)}) copy-start(f32[768]{0:T(1024)} %param.20) | copy-start | bytes 9220
  158.9 66.5 %copy-start.5 = (s32[1,2]{1,0:T(1,128)S(1)}, s32[1,2]{1,0:T(1,128)}, u32[]{:S(2)}) copy-start(s32[1,2]{1,0:T(1,128)} %param.23) | copy-start | bytes 28
  225.5 13.5 %collective-permute-start = (f32[2,1152]{1,0:T(2,128)S(1)}, f32[2,1152]{1,0:T(2,128)S(1)}, u32[]{:S(2)}, u32[]{:S(2)}) collective-permute-start(f32[2,1152]{1,0:T(2,128)S(1)} %copy.20), channel_id=1, source_target_pairs={{0,32},{32,64},{64,96},{96,128},{128,160},{160,192},{192,224},{224... | collective-permute-start | bytes 27656 | tf_op jit(solution)/shard_map/while/body/eval_jaxpr/ppermute | solution.py:12
  230.9 8.0 collective-permute-start.1
  239.0 11.1 %collective-permute-start = (f32[2,1152]{1,0:T(2,128)S(1)}, f32[2,1152]{1,0:T(2,128)S(1)}, u32[]{:S(2)}, u32[]{:S(2)}) collective-permute-start(f32[2,1152]{1,0:T(2,128)S(1)} %copy.20), channel_id=1, source_target_pairs={{0,32},{32,64},{64,96},{96,128},{128,160},{160,192},{192,224},{224... | collective-permute-start | bytes 27656 | tf_op jit(solution)/shard_map/while/body/eval_jaxpr/ppermute | solution.py:12
  242.0 8.0 collective-permute-start.1
  250.1 11.6 %collective-permute-start = (f32[2,1152]{1,0:T(2,128)S(1)}, f32[2,1152]{1,0:T(2,128)S(1)}, u32[]{:S(2)}, u32[]{:S(2)}) collective-permute-start(f32[2,1152]{1,0:T(2,128)S(1)} %copy.20), channel_id=1, source_target_pairs={{0,32},{32,64},{64,96},{96,128},{128,160},{160,192},{192,224},{224... | collective-permute-start | bytes 27656 | tf_op jit(solution)/shard_map/while/body/eval_jaxpr/ppermute | solution.py:12
  253.7 8.0 collective-permute-start.1
  261.7 11.1 %collective-permute-start = (f32[2,1152]{1,0:T(2,128)S(1)}, f32[2,1152]{1,0:T(2,128)S(1)}, u32[]{:S(2)}, u32[]{:S(2)}) collective-permute-start(f32[2,1152]{1,0:T(2,128)S(1)} %copy.20), channel_id=1, source_target_pairs={{0,32},{32,64},{64,96},{96,128},{128,160},{160,192},{192,224},{224... | collective-permute-start | bytes 27656 | tf_op jit(solution)/shard_map/while/body/eval_jaxpr/ppermute | solution.py:12
  264.8 8.0 collective-permute-start.1
  272.8 11.6 %collective-permute-start = (f32[2,1152]{1,0:T(2,128)S(1)}, f32[2,1152]{1,0:T(2,128)S(1)}, u32[]{:S(2)}, u32[]{:S(2)}) collective-permute-start(f32[2,1152]{1,0:T(2,128)S(1)} %copy.20), channel_id=1, source_target_pairs={{0,32},{32,64},{64,96},{96,128},{128,160},{160,192},{192,224},{224... | collective-permute-start | bytes 27656 | tf_op jit(solution)/shard_map/while/body/eval_jaxpr/ppermute | solution.py:12
  276.4 8.0 collective-permute-start.1
  284.4 11.1 %collective-permute-start = (f32[2,1152]{1,0:T(2,128)S(1)}, f32[2,1152]{1,0:T(2,128)S(1)}, u32[]{:S(2)}, u32[]{:S(2)}) collective-permute-start(f32[2,1152]{1,0:T(2,128)S(1)} %copy.20), channel_id=1, source_target_pairs={{0,32},{32,64},{64,96},{96,128},{128,160},{160,192},{192,224},{224... | collective-permute-start | bytes 27656 | tf_op jit(solution)/shard_map/while/body/eval_jaxpr/ppermute | solution.py:12
  287.5 8.0 collective-permute-start.1
  295.5 11.6 %collective-permute-start = (f32[2,1152]{1,0:T(2,128)S(1)}, f32[2,1152]{1,0:T(2,128)S(1)}, u32[]{:S(2)}, u32[]{:S(2)}) collective-permute-start(f32[2,1152]{1,0:T(2,128)S(1)} %copy.20), channel_id=1, source_target_pairs={{0,32},{32,64},{64,96},{96,128},{128,160},{160,192},{192,224},{224... | collective-permute-start | bytes 27656 | tf_op jit(solution)/shard_map/while/body/eval_jaxpr/ppermute | solution.py:12
  299.1 8.0 collective-permute-start.1
  307.1 12.3 %collective-permute-start = (f32[2,1152]{1,0:T(2,128)S(1)}, f32[2,1152]{1,0:T(2,128)S(1)}, u32[]{:S(2)}, u32[]{:S(2)}) collective-permute-start(f32[2,1152]{1,0:T(2,128)S(1)} %copy.20), channel_id=1, source_target_pairs={{0,32},{32,64},{64,96},{96,128},{128,160},{160,192},{192,224},{224... | collective-permute-start | bytes 27656 | tf_op jit(solution)/shard_map/while/body/eval_jaxpr/ppermute | solution.py:12
  311.4 8.0 collective-permute-start.1
  319.4 13.1 %collective-permute-start = (f32[2,1152]{1,0:T(2,128)S(1)}, f32[2,1152]{1,0:T(2,128)S(1)}, u32[]{:S(2)}, u32[]{:S(2)}) collective-permute-start(f32[2,1152]{1,0:T(2,128)S(1)} %copy.20), channel_id=1, source_target_pairs={{0,32},{32,64},{64,96},{96,128},{128,160},{160,192},{192,224},{224... | collective-permute-start | bytes 27656 | tf_op jit(solution)/shard_map/while/body/eval_jaxpr/ppermute | solution.py:12
  324.4 8.0 collective-permute-start.1
  332.5 11.2 %collective-permute-start = (f32[2,1152]{1,0:T(2,128)S(1)}, f32[2,1152]{1,0:T(2,128)S(1)}, u32[]{:S(2)}, u32[]{:S(2)}) collective-permute-start(f32[2,1152]{1,0:T(2,128)S(1)} %copy.20), channel_id=1, source_target_pairs={{0,32},{32,64},{64,96},{96,128},{128,160},{160,192},{192,224},{224... | collective-permute-start | bytes 27656 | tf_op jit(solution)/shard_map/while/body/eval_jaxpr/ppermute | solution.py:12
  335.6 8.0 collective-permute-start.1
  343.7 11.1 %collective-permute-start = (f32[2,1152]{1,0:T(2,128)S(1)}, f32[2,1152]{1,0:T(2,128)S(1)}, u32[]{:S(2)}, u32[]{:S(2)}) collective-permute-start(f32[2,1152]{1,0:T(2,128)S(1)} %copy.20), channel_id=1, source_target_pairs={{0,32},{32,64},{64,96},{96,128},{128,160},{160,192},{192,224},{224... | collective-permute-start | bytes 27656 | tf_op jit(solution)/shard_map/while/body/eval_jaxpr/ppermute | solution.py:12
  346.7 8.0 collective-permute-start.1
  354.7 11.1 %collective-permute-start = (f32[2,1152]{1,0:T(2,128)S(1)}, f32[2,1152]{1,0:T(2,128)S(1)}, u32[]{:S(2)}, u32[]{:S(2)}) collective-permute-start(f32[2,1152]{1,0:T(2,128)S(1)} %copy.20), channel_id=1, source_target_pairs={{0,32},{32,64},{64,96},{96,128},{128,160},{160,192},{192,224},{224... | collective-permute-start | bytes 27656 | tf_op jit(solution)/shard_map/while/body/eval_jaxpr/ppermute | solution.py:12
  357.8 8.0 collective-permute-start.1
  365.8 11.1 %collective-permute-start = (f32[2,1152]{1,0:T(2,128)S(1)}, f32[2,1152]{1,0:T(2,128)S(1)}, u32[]{:S(2)}, u32[]{:S(2)}) collective-permute-start(f32[2,1152]{1,0:T(2,128)S(1)} %copy.20), channel_id=1, source_target_pairs={{0,32},{32,64},{64,96},{96,128},{128,160},{160,192},{192,224},{224... | collective-permute-start | bytes 27656 | tf_op jit(solution)/shard_map/while/body/eval_jaxpr/ppermute | solution.py:12
  368.9 8.0 collective-permute-start.1
  376.9 11.1 %collective-permute-start = (f32[2,1152]{1,0:T(2,128)S(1)}, f32[2,1152]{1,0:T(2,128)S(1)}, u32[]{:S(2)}, u32[]{:S(2)}) collective-permute-start(f32[2,1152]{1,0:T(2,128)S(1)} %copy.20), channel_id=1, source_target_pairs={{0,32},{32,64},{64,96},{96,128},{128,160},{160,192},{192,224},{224... | collective-permute-start | bytes 27656 | tf_op jit(solution)/shard_map/while/body/eval_jaxpr/ppermute | solution.py:12
  380.0 8.0 collective-permute-start.1
  388.0 11.1 %collective-permute-start = (f32[2,1152]{1,0:T(2,128)S(1)}, f32[2,1152]{1,0:T(2,128)S(1)}, u32[]{:S(2)}, u32[]{:S(2)}) collective-permute-start(f32[2,1152]{1,0:T(2,128)S(1)} %copy.20), channel_id=1, source_target_pairs={{0,32},{32,64},{64,96},{96,128},{128,160},{160,192},{192,224},{224... | collective-permute-start | bytes 27656 | tf_op jit(solution)/shard_map/while/body/eval_jaxpr/ppermute | solution.py:12
  391.1 8.0 collective-permute-start.1
  399.1 11.1 %collective-permute-start = (f32[2,1152]{1,0:T(2,128)S(1)}, f32[2,1152]{1,0:T(2,128)S(1)}, u32[]{:S(2)}, u32[]{:S(2)}) collective-permute-start(f32[2,1152]{1,0:T(2,128)S(1)} %copy.20), channel_id=1, source_target_pairs={{0,32},{32,64},{64,96},{96,128},{128,160},{160,192},{192,224},{224... | collective-permute-start | bytes 27656 | tf_op jit(solution)/shard_map/while/body/eval_jaxpr/ppermute | solution.py:12
  402.2 8.0 collective-permute-start.1
  410.2 2.4 copy-start.3
  417.2 1.2 copy-start.6
  421.2 288.2 %all-reduce.55.cloned.1.call-start = ((), (), s32[]{:S(2)}) async-start(), calls=%async_computation.6 | async-start | bytes 147456 | tf_op jit(solution)/shard_map/psum | solution.py:119
  559.3 428.8 %all-reduce.53.cloned.1.call-start = ((), (), s32[]{:S(2)}) async-start(), calls=%async_computation.4 | async-start | bytes 344064 | tf_op jit(solution)/shard_map/psum | solution.py:115
Sparse Core Ops, SparseCore 0:
  10.1 74.2 all-gather.3
  86.5 67.7 all-gather.5
  156.5 66.9 all-gather.7
  421.4 137.8 reduce-scatter.1
  562.0 147.3 all-reduce.54
  715.6 272.4 all-reduce.52
where the time goes:
time: 998 us; the launch traced here: 997 us
  waiting for transfers between devices  774 us (78%)
  starting transfers between devices  104 us (10%)
  other arithmetic  50 us (5%)
  matrix products  44.9 us (4%)
  between operations  15.4 us (2%)
    psum x1, waiting for transfers between devices, body(): kernel_grad = lax.psum(kernel_part, ('loop', 'dp'))  277 us
    psum x1, waiting for transfers between devices, body(): up_grad = lax.psum(up_rows, 'loop').astype(jnp.float32)  149 us
    reduce_scatter x1, waiting for transfers between devices, body(): lax.psum_scatter(up_part.astype(jnp.float32).astype(jnp.bfloat16), 'dp',...  119 us
    ppermute x32, starting transfers between devices, passed_along(): return lax.ppermute(value, axis, pairs)  104 us
    all_gather x1, waiting for transfers between devices, body(): lax.all_gather(w_down, 'dp', axis=0, tiled=True)  65.1 us
    all_gather x1, waiting for transfers between devices, body(): lax.all_gather(w_head, 'dp', axis=0, tiled=True)  64.5 us
    ppermute x32, waiting for transfers between devices, passed_along(): return lax.ppermute(value, axis, pairs)  59.5 us
    all_gather x1, waiting for transfers between devices, body(): lax.all_gather(w_up, 'dp', axis=0, tiled=True)  37.7 us
  transfers between devices with their start and end apart: 38, of which 22 were waited for; matrix products, arithmetic and copies ran while one was open for 9% of the time, Pallas kernels for 0%

commit v1 on v0

--- a/solution.py
+++ b/solution.py
@@ -63,7 +63,9 @@
     loop_size = lax.axis_size("loop")
     loop_index = lax.axis_index("loop")
     up_full, down_full, head_full = (
-        lax.all_gather(w_up, "dp", axis=0, tiled=True),
+        jnp.concatenate(
+            lax.all_to_all(jnp.stack([w_up] * lax.axis_size("dp")), "dp", 0, 0), axis=0
+        ),
         lax.all_gather(w_down, "dp", axis=0, tiled=True),
         lax.all_gather(w_head, "dp", axis=0, tiled=True),
     )

time: 998 us -> 943 us (0.945)
  waiting for transfers between devices: 774 us -> 727 us
  other arithmetic: 50 us -> 30.3 us
  starting transfers between devices: 104 us -> 117 us
    all_gather x1, waiting for transfers between devices: 65.1 us -> 5.96 us  [body(): lax.all_gather(w_down, 'dp', axis=0, tiled=True)]
    all_to_all x0 -> x1, waiting for transfers between devices: none -> 51.5 us  [body(): lax.all_to_all(jnp.stack([w_up] * lax.axis_size('dp')), 'dp', 0, 0)]
    all_gather x1 -> x0, waiting for transfers between devices: 37.7 us -> none  [body(): lax.all_gather(w_up, 'dp', axis=0, tiled=True)]
    reduce_sum x1, other arithmetic: 30.5 us -> 12.2 us  [image_tower(): chan_mean = jnp.mean(conv_out, axis=-1, keepdims=True)]
    all_to_all x0 -> x1, starting transfers between devices: none -> 13.1 us  [body(): lax.all_to_all(jnp.stack([w_up] * lax.axis_size('dp')), 'dp', 0, 0)]
  transfers between devices with their start and end apart: 38 -> 38, of which waited for: 22 -> 22; matrix products, arithmetic and copies ran while one was open for 9% -> 7% of each run, Pallas kernels for 0% -> 0%
where the time goes in v1:
time: 943 us; the launch traced here: 941 us
  waiting for transfers between devices  727 us (77%)
  starting transfers between devices  117 us (12%)
  matrix products  44.7 us (5%)
  other arithmetic  30.3 us (3%)
  between operations  15.1 us (2%)
    psum x1, waiting for transfers between devices, body(): kernel_grad = lax.psum(kernel_part, ('loop', 'dp'))  277 us
    psum x1, waiting for transfers between devices, body(): up_grad = lax.psum(up_rows, 'loop').astype(jnp.float32)  149 us
    reduce_scatter x1, waiting for transfers between devices, body(): lax.psum_scatter(up_part.astype(jnp.float32).astype(jnp.bfloat16), 'dp',...  119 us
    ppermute x32, starting transfers between devices, passed_along(): return lax.ppermute(value, axis, pairs)  104 us
    all_gather x1, waiting for transfers between devices, body(): lax.all_gather(w_head, 'dp', axis=0, tiled=True)  63.8 us
    ppermute x32, waiting for transfers between devices, passed_along(): return lax.ppermute(value, axis, pairs)  59.3 us
    all_to_all x1, waiting for transfers between devices, body(): lax.all_to_all(jnp.stack([w_up] * lax.axis_size('dp')), 'dp', 0, 0)  51.5 us
  transfers between devices with their start and end apart: 38, of which 22 were waited for; matrix products, arithmetic and copies ran while one was open for 7% of the time, Pallas kernels for 0%

profile of v1, /device:TPU:1, one launch (start us, length us, event | category | flops | bytes accessed | tf_op | source)
XLA Modules:
  0.0 941.5 jit_solution(7984755340041012795)
XLA Ops:
  10.4 13.1 %all-to-all-start = ((bf16[32,24,1536]{2,1,0:T(8,128)(2,1)}), bf16[32,24,1536]{2,1,0:T(8,128)(2,1)}, u32[]{:S(2)}, u32[]{:S(2)}) async-start(bf16[32,24,1536]{2,1,0:T(8,128)(2,1)} %stack.2), calls=%async_computation | async-start | bytes 4718592 | tf_op jit(solution)/shard_map/all_to_all | solution.py:67
  25.7 12.2 %fusion.140 = (f32[2,16,16]{2,1,0:T(8,128)S(1)}, f32[2,16,16,768]{3,2,1,0:T(8,128)S(1)}) fusion(f32[768]{0:T(1024)S(1)} %get-tuple-element.377, f32[768]{0:T(1024)S(1)} %get-tuple-element.378, f32[768]{0:T(1024)S(1)} %get-tuple-element.331, f32[768]{0:T(1024)S(1)} %get-tuple-element.332, f32[768]{0:T(1024)S(1)} %get-tuple-element.333, ...), kind=kLoop, calls=%fused_computation.374 | loop fusion | flops 57802240 | bytes 2511872 | tf_op jit(solution)/shard_map/jvp()/reduce_sum | solution.py:25
  38.5 51.5 %all-to-all-done = bf16[32,24,1536]{2,1,0:T(8,128)(2,1)} async-done(((bf16[32,24,1536]{2,1,0:T(8,128)(2,1)}), bf16[32,24,1536]{2,1,0:T(8,128)(2,1)}, u32[]{:S(2)}, u32[]{:S(2)}) %all-to-all-start) | async-done | bytes 2359328 | tf_op jit(solution)/shard_map/all_to_all | solution.py:67
  89.9 4.7 convolution_add_fusion
  94.7 6.0 all-gather.3.cloned.1.call-done
  100.6 4.6 bitcast_reduce_fusion
  105.3 63.8 %all-gather.5.cloned.1.call-done = bf16[768,1152]{1,0:T(8,128)(2,1)} async-done(((bf16[24,1152]{1,0:T(8,128)(2,1)}), bf16[768,1152]{1,0:T(8,128)(2,1)}) %all-gather.5.cloned.1.call-update) | async-done | bytes 1769488 | tf_op jit(solution)/shard_map/all_gather | solution.py:70
  171.1 184.7 %while.20 = (s32[]{:T(128)}, f32[2,1152]{1,0:T(2,128)S(1)}, f32[2,1152]{1,0:T(2,128)S(1)}, f32[2,1152]{1,0:T(2,128)S(1)}, f32[]{:T(128)}, /*index=5*/s32[1,2]{1,...) while((s32[]{:T(128)}, f32[2,1152]{1,0:T(2,128)S(1)}, ...), condition=%wide.region_6.7_spmd.clone, body=%wide.region_5.6_spmd.clone.sunk | while | flops 177470 | bytes 166336 | solution.py:112
  171.2 4.3 collective-permute-start
  176.6 3.4 collective-permute-start.1
  180.2 4.4 collective-permute-done.1
  187.7 4.6 collective-permute-start.1
  192.5 3.2 collective-permute-done.1
  199.4 3.4 collective-permute-start.1
  203.0 4.4 collective-permute-done.1
  210.5 4.6 collective-permute-start.1
  215.2 3.2 collective-permute-done.1
  222.1 3.4 collective-permute-start.1
  225.7 4.4 collective-permute-done.1
  233.2 4.6 collective-permute-start.1
  238.0 3.2 collective-permute-done.1
  244.8 5.2 collective-permute-start.1
  257.1 6.0 collective-permute-start.1
  265.1 3.9 collective-permute-start
  270.1 3.9 collective-permute-start.1
  274.2 4.0 collective-permute-done.1
  281.3 3.8 collective-permute-start.1
  285.3 4.0 collective-permute-done.1
  292.4 3.8 collective-permute-start.1
  296.4 4.0 collective-permute-done.1
  303.5 3.8 collective-permute-start.1
  307.5 4.0 collective-permute-done.1
  314.6 3.8 collective-permute-start.1
  318.6 4.0 collective-permute-done.1
  325.7 3.8 collective-permute-start.1
  329.7 4.0 collective-permute-done.1
  336.8 3.8 collective-permute-start.1
  340.7 4.0 collective-permute-done.1
  347.8 4.2 collective-permute-start.1
  352.2 3.7 collective-permute-done.1
  358.3 4.4 fusion.14
  367.0 3.6 fusion.143
  371.6 5.0 fusion.117
  376.8 3.7 fusion.23
  380.5 3.9 fusion.118
  385.8 118.9 %reduce-scatter.2.cloned.1.call-done = bf16[24,1536]{1,0:T(8,128)(2,1)} async-done(((bf16[768,1536]{1,0:T(8,128)(2,1)}), bf16[24,1536]{1,0:T(8,128)(2,1)}) %reduce-scatter.2.cloned.1.call-update) | async-done | bytes 73744 | tf_op jit(solution)/shard_map/reduce_scatter | solution.py:118
  506.0 148.7 %all-reduce.55.cloned.1.call-done = bf16[24,1536]{1,0:T(8,128)(2,1)} async-done(((bf16[24,1536]{1,0:T(8,128)(2,1)}), bf16[24,1536]{1,0:T(8,128)(2,1)}) %all-reduce.55.cloned.1.call-update) | async-done | bytes 73744 | tf_op jit(solution)/shard_map/psum | solution.py:121
  656.3 277.1 %all-reduce.53.cloned.1.call-done = f32[7,7,768]{2,1,0:T(8,128)} async-done(((f32[7,7,768]{2,1,0:T(8,128)}), f32[7,7,768]{2,1,0:T(8,128)}) %all-reduce.53.cloned.1.call-update) | async-done | bytes 150544 | tf_op jit(solution)/shard_map/psum | solution.py:117
  (220 shorter events, 75.2 us)
Async XLA Ops:
  7.2 93.5 %all-gather.3.cloned.1.call-start = ((), (), s32[]{:S(2)}) async-start(), calls=%async_computation.2 | async-start | bytes 2433024 | tf_op jit(solution)/shard_map/all_gather | solution.py:69
  10.3 14.6 %copy-start.3 = (bf16[1,2,1152]{2,1,0:T(2,128)(2,1)S(1)}, bf16[1,2,1152]{2,1,0:T(2,128)(2,1)}, u32[]{:S(2)}) copy-start(bf16[1,2,1152]{2,1,0:T(2,128)(2,1)} %param.22) | copy-start | bytes 13828
  10.3 14.8 %copy-start.1 = (f32[7,7,768]{2,1,0:T(8,128)S(1)}, f32[7,7,768]{2,1,0:T(8,128)}, u32[]{:S(2)}) copy-start(f32[7,7,768]{2,1,0:T(8,128)} %param.15) | copy-start | bytes 451588
  10.4 15.3 %copy-start = (bf16[1,2,16,16,768]{4,3,2,1,0:T(8,128)(2,1)S(1)}, bf16[1,2,16,16,768]{4,3,2,1,0:T(8,128)(2,1)}, u32[]{:S(2)}) copy-start(bf16[1,2,16,16,768]{4,3,2,1,0:T(8,128)(2,1)} %param.14) | copy-start | bytes 2359300
  10.4 79.6 %all-to-all-start = ((bf16[32,24,1536]{2,1,0:T(8,128)(2,1)}), bf16[32,24,1536]{2,1,0:T(8,128)(2,1)}, u32[]{:S(2)}, u32[]{:S(2)}) async-start(bf16[32,24,1536]{2,1,0:T(8,128)(2,1)} %stack.2), calls=%async_computation | async-start | bytes 4718592 | tf_op jit(solution)/shard_map/all_to_all | solution.py:67
  23.4 145.7 %all-gather.5.cloned.1.call-start = ((), (), s32[]{:S(2)}) async-start(), calls=%async_computation.3 | async-start | bytes 1824768 | tf_op jit(solution)/shard_map/all_gather | solution.py:70
  24.2 480.5 %reduce-scatter.2.cloned.1.call-start = ((), (), s32[]{:S(2)}) async-start(), calls=%async_computation.5 | async-start | bytes 2433024 | tf_op jit(solution)/shard_map/reduce_scatter | solution.py:118
  25.7 12.5 %copy-start.2 = (f32[768]{0:T(1024)S(1)}, f32[768]{0:T(1024)}, u32[]{:S(2)}) copy-start(f32[768]{0:T(1024)} %param.16) | copy-start | bytes 9220
  38.2 51.8 %copy-start.6 = (f32[1536]{0:T(1024)S(1)}, f32[1536]{0:T(1024)}, u32[]{:S(2)}) copy-start(f32[1536]{0:T(1024)} %param.18) | copy-start | bytes 18436
  89.9 10.7 %copy-start.4 = (f32[768]{0:T(1024)S(1)}, f32[768]{0:T(1024)}, u32[]{:S(2)}) copy-start(f32[768]{0:T(1024)} %param.20) | copy-start | bytes 9220
  105.2 65.9 %copy-start.7 = (s32[1,2]{1,0:T(1,128)S(1)}, s32[1,2]{1,0:T(1,128)}, u32[]{:S(2)}) copy-start(s32[1,2]{1,0:T(1,128)} %param.23) | copy-start | bytes 28
  171.2 13.5 %collective-permute-start = (f32[2,1152]{1,0:T(2,128)S(1)}, f32[2,1152]{1,0:T(2,128)S(1)}, u32[]{:S(2)}, u32[]{:S(2)}) collective-permute-start(f32[2,1152]{1,0:T(2,128)S(1)} %copy.20), channel_id=1, source_target_pairs={{0,32},{32,64},{64,96},{96,128},{128,160},{160,192},{192,224},{224... | collective-permute-start | bytes 27656 | tf_op jit(solution)/shard_map/while/body/eval_jaxpr/ppermute | solution.py:12
  176.6 8.0 collective-permute-start.1
  184.7 11.1 %collective-permute-start = (f32[2,1152]{1,0:T(2,128)S(1)}, f32[2,1152]{1,0:T(2,128)S(1)}, u32[]{:S(2)}, u32[]{:S(2)}) collective-permute-start(f32[2,1152]{1,0:T(2,128)S(1)} %copy.20), channel_id=1, source_target_pairs={{0,32},{32,64},{64,96},{96,128},{128,160},{160,192},{192,224},{224... | collective-permute-start | bytes 27656 | tf_op jit(solution)/shard_map/while/body/eval_jaxpr/ppermute | solution.py:12
  187.7 8.0 collective-permute-start.1
  195.8 11.6 %collective-permute-start = (f32[2,1152]{1,0:T(2,128)S(1)}, f32[2,1152]{1,0:T(2,128)S(1)}, u32[]{:S(2)}, u32[]{:S(2)}) collective-permute-start(f32[2,1152]{1,0:T(2,128)S(1)} %copy.20), channel_id=1, source_target_pairs={{0,32},{32,64},{64,96},{96,128},{128,160},{160,192},{192,224},{224... | collective-permute-start | bytes 27656 | tf_op jit(solution)/shard_map/while/body/eval_jaxpr/ppermute | solution.py:12
  199.4 8.0 collective-permute-start.1
  207.4 11.1 %collective-permute-start = (f32[2,1152]{1,0:T(2,128)S(1)}, f32[2,1152]{1,0:T(2,128)S(1)}, u32[]{:S(2)}, u32[]{:S(2)}) collective-permute-start(f32[2,1152]{1,0:T(2,128)S(1)} %copy.20), channel_id=1, source_target_pairs={{0,32},{32,64},{64,96},{96,128},{128,160},{160,192},{192,224},{224... | collective-permute-start | bytes 27656 | tf_op jit(solution)/shard_map/while/body/eval_jaxpr/ppermute | solution.py:12
  210.5 8.0 collective-permute-start.1
  218.5 11.6 %collective-permute-start = (f32[2,1152]{1,0:T(2,128)S(1)}, f32[2,1152]{1,0:T(2,128)S(1)}, u32[]{:S(2)}, u32[]{:S(2)}) collective-permute-start(f32[2,1152]{1,0:T(2,128)S(1)} %copy.20), channel_id=1, source_target_pairs={{0,32},{32,64},{64,96},{96,128},{128,160},{160,192},{192,224},{224... | collective-permute-start | bytes 27656 | tf_op jit(solution)/shard_map/while/body/eval_jaxpr/ppermute | solution.py:12
  222.1 8.0 collective-permute-start.1
  230.1 11.1 %collective-permute-start = (f32[2,1152]{1,0:T(2,128)S(1)}, f32[2,1152]{1,0:T(2,128)S(1)}, u32[]{:S(2)}, u32[]{:S(2)}) collective-permute-start(f32[2,1152]{1,0:T(2,128)S(1)} %copy.20), channel_id=1, source_target_pairs={{0,32},{32,64},{64,96},{96,128},{128,160},{160,192},{192,224},{224... | collective-permute-start | bytes 27656 | tf_op jit(solution)/shard_map/while/body/eval_jaxpr/ppermute | solution.py:12
  233.2 8.0 collective-permute-start.1
  241.2 11.6 %collective-permute-start = (f32[2,1152]{1,0:T(2,128)S(1)}, f32[2,1152]{1,0:T(2,128)S(1)}, u32[]{:S(2)}, u32[]{:S(2)}) collective-permute-start(f32[2,1152]{1,0:T(2,128)S(1)} %copy.20), channel_id=1, source_target_pairs={{0,32},{32,64},{64,96},{96,128},{128,160},{160,192},{192,224},{224... | collective-permute-start | bytes 27656 | tf_op jit(solution)/shard_map/while/body/eval_jaxpr/ppermute | solution.py:12
  244.8 8.0 collective-permute-start.1
  252.8 12.2 %collective-permute-start = (f32[2,1152]{1,0:T(2,128)S(1)}, f32[2,1152]{1,0:T(2,128)S(1)}, u32[]{:S(2)}, u32[]{:S(2)}) collective-permute-start(f32[2,1152]{1,0:T(2,128)S(1)} %copy.20), channel_id=1, source_target_pairs={{0,32},{32,64},{64,96},{96,128},{128,160},{160,192},{192,224},{224... | collective-permute-start | bytes 27656 | tf_op jit(solution)/shard_map/while/body/eval_jaxpr/ppermute | solution.py:12
  257.1 8.0 collective-permute-start.1
  265.1 13.1 %collective-permute-start = (f32[2,1152]{1,0:T(2,128)S(1)}, f32[2,1152]{1,0:T(2,128)S(1)}, u32[]{:S(2)}, u32[]{:S(2)}) collective-permute-start(f32[2,1152]{1,0:T(2,128)S(1)} %copy.20), channel_id=1, source_target_pairs={{0,32},{32,64},{64,96},{96,128},{128,160},{160,192},{192,224},{224... | collective-permute-start | bytes 27656 | tf_op jit(solution)/shard_map/while/body/eval_jaxpr/ppermute | solution.py:12
  270.1 8.0 collective-permute-start.1
  278.2 11.2 %collective-permute-start = (f32[2,1152]{1,0:T(2,128)S(1)}, f32[2,1152]{1,0:T(2,128)S(1)}, u32[]{:S(2)}, u32[]{:S(2)}) collective-permute-start(f32[2,1152]{1,0:T(2,128)S(1)} %copy.20), channel_id=1, source_target_pairs={{0,32},{32,64},{64,96},{96,128},{128,160},{160,192},{192,224},{224... | collective-permute-start | bytes 27656 | tf_op jit(solution)/shard_map/while/body/eval_jaxpr/ppermute | solution.py:12
  281.3 8.0 collective-permute-start.1
  289.3 11.1 %collective-permute-start = (f32[2,1152]{1,0:T(2,128)S(1)}, f32[2,1152]{1,0:T(2,128)S(1)}, u32[]{:S(2)}, u32[]{:S(2)}) collective-permute-start(f32[2,1152]{1,0:T(2,128)S(1)} %copy.20), channel_id=1, source_target_pairs={{0,32},{32,64},{64,96},{96,128},{128,160},{160,192},{192,224},{224... | collective-permute-start | bytes 27656 | tf_op jit(solution)/shard_map/while/body/eval_jaxpr/ppermute | solution.py:12
  292.4 8.0 collective-permute-start.1
  300.4 11.1 %collective-permute-start = (f32[2,1152]{1,0:T(2,128)S(1)}, f32[2,1152]{1,0:T(2,128)S(1)}, u32[]{:S(2)}, u32[]{:S(2)}) collective-permute-start(f32[2,1152]{1,0:T(2,128)S(1)} %copy.20), channel_id=1, source_target_pairs={{0,32},{32,64},{64,96},{96,128},{128,160},{160,192},{192,224},{224... | collective-permute-start | bytes 27656 | tf_op jit(solution)/shard_map/while/body/eval_jaxpr/ppermute | solution.py:12
  303.5 8.0 collective-permute-start.1
  311.5 11.1 %collective-permute-start = (f32[2,1152]{1,0:T(2,128)S(1)}, f32[2,1152]{1,0:T(2,128)S(1)}, u32[]{:S(2)}, u32[]{:S(2)}) collective-permute-start(f32[2,1152]{1,0:T(2,128)S(1)} %copy.20), channel_id=1, source_target_pairs={{0,32},{32,64},{64,96},{96,128},{128,160},{160,192},{192,224},{224... | collective-permute-start | bytes 27656 | tf_op jit(solution)/shard_map/while/body/eval_jaxpr/ppermute | solution.py:12
  314.6 8.0 collective-permute-start.1
  322.6 11.1 %collective-permute-start = (f32[2,1152]{1,0:T(2,128)S(1)}, f32[2,1152]{1,0:T(2,128)S(1)}, u32[]{:S(2)}, u32[]{:S(2)}) collective-permute-start(f32[2,1152]{1,0:T(2,128)S(1)} %copy.20), channel_id=1, source_target_pairs={{0,32},{32,64},{64,96},{96,128},{128,160},{160,192},{192,224},{224... | collective-permute-start | bytes 27656 | tf_op jit(solution)/shard_map/while/body/eval_jaxpr/ppermute | solution.py:12
  325.7 8.0 collective-permute-start.1
  333.7 11.1 %collective-permute-start = (f32[2,1152]{1,0:T(2,128)S(1)}, f32[2,1152]{1,0:T(2,128)S(1)}, u32[]{:S(2)}, u32[]{:S(2)}) collective-permute-start(f32[2,1152]{1,0:T(2,128)S(1)} %copy.20), channel_id=1, source_target_pairs={{0,32},{32,64},{64,96},{96,128},{128,160},{160,192},{192,224},{224... | collective-permute-start | bytes 27656 | tf_op jit(solution)/shard_map/while/body/eval_jaxpr/ppermute | solution.py:12
  336.8 8.0 collective-permute-start.1
  344.8 11.1 %collective-permute-start = (f32[2,1152]{1,0:T(2,128)S(1)}, f32[2,1152]{1,0:T(2,128)S(1)}, u32[]{:S(2)}, u32[]{:S(2)}) collective-permute-start(f32[2,1152]{1,0:T(2,128)S(1)} %copy.20), channel_id=1, source_target_pairs={{0,32},{32,64},{64,96},{96,128},{128,160},{160,192},{192,224},{224... | collective-permute-start | bytes 27656 | tf_op jit(solution)/shard_map/while/body/eval_jaxpr/ppermute | solution.py:12
  347.8 8.0 collective-permute-start.1
  355.9 2.4 copy-start.5
  362.7 1.2 copy-start.8
  366.8 287.9 %all-reduce.55.cloned.1.call-start = ((), (), s32[]{:S(2)}) async-start(), calls=%async_computation.6 | async-start | bytes 147456 | tf_op jit(solution)/shard_map/psum | solution.py:121
  504.7 428.6 %all-reduce.53.cloned.1.call-start = ((), (), s32[]{:S(2)}) async-start(), calls=%async_computation.4 | async-start | bytes 344064 | tf_op jit(solution)/shard_map/psum | solution.py:117
Sparse Core Ops, SparseCore 0:
  10.1 90.4 all-gather.2
  102.8 66.2 all-gather.4
  366.9 137.7 reduce-scatter.1
  507.5 147.1 all-reduce.54
  660.9 272.4 all-reduce.52
